TPU v7x, 32 devices: a whole 2x2x4 slice. The times are simulated.
32 devices in a mesh: section: 4 (over y, core), dp: 8 (over z, x).
Axes of the slice: x: 2, y: 2, z: 4, core: 2. Of those that a mesh axis runs over, the one named last changes fastest.
Arguments:
- queries: bfloat16 [4, 1024, 8192], P('section', 'dp'), may hold values from -48 to 48
- image_kv: bfloat16 [4, 2, 32, 1024], P(None, None, ('section', 'dp')), may hold values from -4 to 4
- visible: int32 [1024], P('dp'), may hold values from 0 to 32, as said below
- gate: float32 [4], P('section'), may hold values from 0.3 to 2
Outputs:
- cross_out: bfloat16 [4, 1024, 8192], P('section', 'dp')
Inputs may be any that keep to these rules, and one draw needn't show every extreme that they name: `visible`: every value is a multiple of 8; the last token of each aligned block of 128 text tokens sees all 32 image tokens.
All inputs are finite; a program needn't handle non-finite values.
Results may differ from a plain program's by a relative error of at most 0.0065.
Values may be sent and summed in bfloat16 or wider, within the bound.
A program may use at most 64 MiB of HBM per device.

v0:
```python
import math

import jax
import jax.numpy as jnp
from jax import lax
from jax.sharding import PartitionSpec as P

H = 64
KVH = 8
HD = 128


block_rows = 128


def global_position(position, dp_count, section_count, img_dev):
    per_dp = section_count * img_dev
    source_section = position % per_dp // img_dev
    source_dp = position // per_dp
    return source_section * (dp_count * img_dev) + source_dp * img_dev + position % img_dev


def attend(stats, keys_flat, vals_flat, glob, query, seen):
    top, denom, acc = stats
    count = keys_flat.shape[0]
    kv_heads = query.shape[1]
    head_size = query.shape[3]
    keys = keys_flat.reshape(count, kv_heads, head_size)
    vals = vals_flat.reshape(count, kv_heads, head_size)
    live = glob[None, :] < seen[:, None]
    scores = jnp.einsum("tkgd,nkd->kgtn", query, keys, preferred_element_type=jnp.float32)
    scores = scores / jnp.sqrt(jnp.float32(head_size))
    capped = jnp.where(live, scores, -1e30)
    top_new = jnp.maximum(top, jnp.max(capped, axis=-1))
    expo = jnp.where(live, jnp.exp(capped - top_new[..., None]), 0.0)
    factor = jnp.exp(top - top_new)
    denom = denom * factor + jnp.sum(expo, axis=-1)
    acc = acc * factor[..., None] + jnp.einsum(
        "kgtn,nkd->kgtd", expo.astype(jnp.bfloat16), vals, preferred_element_type=jnp.float32
    )
    return (top_new, denom, acc)


def body(queries, image_kv, visible, gate):
    section_count = lax.axis_size("section")
    dp_count = lax.axis_size("dp")
    img_dev = image_kv.shape[2]
    rows = queries.shape[1]
    kv_heads = KVH
    groups = H // KVH
    width = image_kv.shape[3]
    query = queries[0].reshape(rows, kv_heads, groups, HD)
    mine = lax.all_to_all(image_kv, "section", split_axis=0, concat_axis=2, tiled=True)
    start_top = jnp.full((kv_heads, groups, rows), -1e30, jnp.float32)
    start_denom = jnp.zeros((kv_heads, groups, rows), jnp.float32)
    start_acc = jnp.zeros((kv_heads, groups, rows, HD), jnp.float32)
    stats = (start_top, start_denom, start_acc)
    whole = lax.all_gather(mine, "dp", axis=2, tiled=True)
    total = whole.shape[2]
    block = math.gcd(total, block_rows)
    count = total // block
    blocked = jnp.moveaxis(whole.reshape(2, count, block, width), 1, 0)

    def scan_step(carry, pair):
        glob = global_position(
            pair[1] + jnp.arange(block, dtype=jnp.int32), dp_count, section_count, img_dev
        )
        return (attend(carry, pair[0][0], pair[0][1], glob, query, visible), None)

    starts = jnp.arange(count, dtype=jnp.int32) * block
    final, unused = lax.scan(scan_step, stats, (blocked, starts))
    top, denom, acc = final
    result = acc / jnp.where(denom > 0, denom, 1.0)[..., None]
    result = jnp.transpose(result, (2, 0, 1, 3)).reshape(rows, H * HD)
    result = jnp.where((visible > 0)[:, None], result, 0.0) * jnp.tanh(gate[0])
    return result.astype(jnp.bfloat16)[None]


def solution(mesh):
    in_specs = (
        P("section", "dp", None),
        P(None, None, ("section", "dp"), None),
        P("dp"),
        P("section"),
    )
    out_specs = P("section", "dp", None)
    return jax.shard_map(body, mesh=mesh, in_specs=in_specs, out_specs=out_specs, check_vma=False)
```

profile of v0, /device:TPU:0, one launch (start us, length us, event | category | flops | bytes accessed | tf_op | source)
XLA Modules:
  0.0 54.7 jit_solution(8085909077950708755)
XLA Ops:
  0.0 4.2 %all-to-all-start = ((bf16[4,2,1,1024]{3,1,2,0:T(2,128)(2,1)}), bf16[4,2,1,1024]{3,1,2,0:T(2,128)(2,1)S(1)}, u32[]{:S(2)}, u32[]{:S(2)}) async-start(bf16[4,2,1,1024]{3,1,2,0:T(2,128)(2,1)} %param.5), calls=%async_computation | async-start | bytes 32768 | tf_op jit(solution)/shard_map/all_to_all | solution.py:53
  4.2 0.7 %broadcast_compare_fusion = pred[128,32]{0,1:T(8,128)(4,1)S(1)} fusion(s32[128]{0:T(128)} %param.6, s32[32]{0:T(128)S(1)} %fusion.21), kind=kLoop, calls=%fused_computation.22 | loop fusion | flops 4096 | bytes 4736 | tf_op jit(solution)/shard_map/while/body/eval_jaxpr/lt | solution.py:30
  5.0 0.7 %broadcast_compare_fusion.1 = pred[128]{0:T(512)(128)(4,1)S(1)} fusion(s32[128]{0:T(128)} %param.6), kind=kLoop, calls=%fused_computation.30 | loop fusion | flops 128 | bytes 640 | tf_op jit(solution)/shard_map/gt | solution.py:75
  5.6 2.2 %copy.28 = bf16[16,8,64,128]{3,2,1,0:T(8,128)(2,1)S(1)} copy(bf16[16,8,64,128]{3,1,2,0:T(8,128)(2,1)} %bitcast.38) | data formatting | bytes 4194304
  8.5 0.0 all-to-all-done
  8.5 31.4 %all-gather = bf16[1,2,32,1,1024]{4,1,3,0,2:T(2,128)(2,1)S(1)} all-gather(bf16[1,2,4,1,1024]{4,1,3,0,2:T(2,128)(2,1)S(1)} %bitcast.43), channel_id=2, replica_groups=mesh['section'=4,'dp'=8] {'dp'}, dimensions={2}, use_global_device_ids=true | all-gather | bytes 147456 | tf_op jit(solution)/shard_map/all_gather | solution.py:58
  39.9 0.5 slice_reduce_fusion
  40.5 1.5 %fusion.23 = (f32[8,8,128]{2,1,0:T(8,128)S(1)}, f32[8,8,128,32]{2,3,1,0:T(8,128)S(1)}) fusion(bf16[128,8,8,128]{3,2,1,0:T(8,128)(2,1)S(1)} %bitcast.36, bf16[32,8,128,1]{2,1,0,3:T(8,128)(2,1)S(1)} %bitcast.40, pred[128,32]{0,1:T(8,128)(4,1)S(1)} %broadcast_compare_fusion), kind=kOutput, calls=%fused_computation.32 | convolution fusion | flops 67887104 | bytes 3248128 | tf_op jit(solution)/shard_map/while/body/eval_jaxpr/tkgd,nkd->kgtn/dot_general | solution.py:31
  42.0 0.3 fusion.12
  42.3 2.7 %fusion = f32[128,8,8,128]{0,3,2,1:T(8,128)} fusion(f32[128,8,8]{0,2,1:T(8,128)S(1)} %compare_select_fusion, f32[128,8,8]{0,2,1:T(8,128)S(1)} %get-tuple-element.19, f32[8,8,128,32]{2,3,1,0:T(8,128)S(1)} %get-tuple-element.30, f32[8,8,128]{2,1,0:T(8,128)S(1)} %get-tuple-element.20, pred[128,32]{0,1:T(8,128)(4,1)S(1)} %broadcast_compare_fusion, ...), kind=kOutput, calls=%fused_computation.1 | convolution fusion | flops 69992448 | bytes 5410816 | tf_op jit(solution)/shard_map/while/body/eval_jaxpr/kgtn,nkd->kgtd/dot_general | solution.py:38
  45.1 5.6 %copy.20 = f32[1,128,8192]{2,1,0:T(8,128)} copy(f32[1,128,8192]{1,2,0:T(8,128)} %bitcast.37) | data formatting | bytes 8388608 | tf_op jit(solution)/shard_map/reshape | solution.py:74
  50.7 4.0 %multiply_convert_fusion = bf16[1,128,8192]{2,1,0:T(8,128)(2,1)} fusion(f32[1,128,8192]{2,1,0:T(8,128)} %copy.20, f32[]{:T(128)} %bitcast.11, pred[128]{0:T(512)(128)(4,1)S(1)} %broadcast_compare_fusion.1), kind=kLoop, calls=%fused_computation.2 | loop fusion | flops 3145728 | bytes 6291588 | tf_op jit(solution)/shard_map/convert_element_type | solution.py:76
  (5 shorter events, 0.1 us)
Async XLA Ops:
  0.0 8.5 %all-to-all-start = ((bf16[4,2,1,1024]{3,1,2,0:T(2,128)(2,1)}), bf16[4,2,1,1024]{3,1,2,0:T(2,128)(2,1)S(1)}, u32[]{:S(2)}, u32[]{:S(2)}) async-start(bf16[4,2,1,1024]{3,1,2,0:T(2,128)(2,1)} %param.5), calls=%async_computation | async-start | bytes 32768 | tf_op jit(solution)/shard_map/all_to_all | solution.py:53
where the time goes:
time: 55.1 us; the launch traced here: 54.7 us
  blocking collectives  31.4 us (57%)
  local copies, waits for them, and re-layouts  8.36 us (15%)
  other arithmetic  5.7 us (10%)
  starting transfers between devices  4.24 us (8%)
  matrix products  4.23 us (8%)
  between operations  0.76 us (1%)
    all_gather x1, blocking collectives, body(): whole = lax.all_gather(mine, 'dp', axis=2, tiled=True)  31.4 us
    reshape x1, local copies, waits for them, and re-layouts, body(): result = jnp.transpose(result, (2, 0, 1, 3)).reshape(rows, H * HD)  5.63 us
    all_to_all x1, starting transfers between devices, body(): lax.all_to_all(image_kv, 'section', split_axis=0, concat_axis=2, tiled=True)  4.24 us
    convert_element_type x1, other arithmetic, body(): return result.astype(jnp.bfloat16)[None]  3.99 us
    dot_general x1, matrix products, attend(): jnp.einsum('kgtn,nkd->kgtd', expo.astype(jnp.bfloat16), vals, preferred_e...  2.73 us
    unnamed x3, local copies, waits for them, and re-layouts  2.2 us
    dot_general x1, matrix products, attend(): jnp.einsum('tkgd,nkd->kgtn', query, keys, preferred_element_type=jnp.floa...  1.5 us
  transfers between devices with their start and end apart: 1, of which 0 were waited for; matrix products, arithmetic and copies ran while one was open for 7% of the time, Pallas kernels for 0%

commit v1 on v0

v1 whole, which is shorter than its diff:
```python
import functools
import math

import jax
import jax.numpy as jnp
from jax import lax
from jax.experimental import pallas as pl
from jax.experimental.pallas import tpu as pltpu
from jax.sharding import PartitionSpec as P

HD = 128
LOG2E = math.log2(math.e)


def gather_kernel(sections, dps, kv_ref, out_ref, stage, send, slots, wide, send_sem, recv_sem):
    count = sections * dps
    my_section = lax.axis_index("section")
    my_dp = lax.axis_index("dp")
    me = my_section * dps + my_dp
    img_dev = kv_ref.shape[1]
    heads = kv_ref.shape[3] // HD
    per_token = 2 * heads
    tokens = count * img_dev

    barrier = pltpu.get_barrier_semaphore()

    def peer_of(step):
        peer = lax.rem(me + step, count)
        return lax.div(peer, dps), lax.rem(peer, dps)

    def greet(step, unused):
        section, dp = peer_of(step)
        pl.semaphore_signal(barrier, inc=1, device_id={"section": section, "dp": dp})
        return unused

    lax.fori_loop(1, count, greet, 0)

    for layer in range(sections):
        for token in range(img_dev):
            rows = kv_ref[layer, token].astype(jnp.float32)
            for part in range(2):
                for head in range(heads):
                    at = token * per_token + part * heads + head
                    stage[layer, at : at + 1, :] = rows[part : part + 1, head * HD : (head + 1) * HD]
        send[layer] = stage[layer].astype(send.dtype)

    pl.semaphore_wait(barrier, count - 1)

    def post(step, unused):
        section, dp = peer_of(step)
        pltpu.make_async_remote_copy(
            src_ref=send.at[section],
            dst_ref=slots.at[me],
            send_sem=send_sem,
            recv_sem=recv_sem,
            device_id={"section": section, "dp": dp},
        ).start()
        return unused

    lax.fori_loop(1, count, post, 0)
    pltpu.make_async_copy(send.at[my_section], slots.at[me], recv_sem).start()
    pltpu.make_async_copy(slots, slots, recv_sem).wait()

    wide[...] = slots[...].reshape(tokens * per_token, HD).astype(jnp.float32)
    for row in range(per_token):
        out_ref[row] = wide[pl.ds(row, tokens, stride=per_token), :].astype(out_ref.dtype)

    others = slots.at[pl.ds(0, count - 1)]
    pltpu.make_async_copy(others, others, send_sem).wait()


def attend_kernel(q_ref, kv_ref, seen_ref, gate_ref, out_ref):
    head = pl.program_id(0)
    heads = kv_ref.shape[0] // 2
    tokens = kv_ref.shape[1]
    rows = q_ref.shape[0]
    keys = kv_ref[head]
    vals = kv_ref[heads + head]
    seen = seen_ref[...]
    live = lax.broadcasted_iota(jnp.int32, (tokens, rows), 0) < seen
    gain = jnp.where(seen > 0, jnp.tanh(gate_ref[...]), 0.0)
    factor = LOG2E / math.sqrt(HD)
    for group in range(q_ref.shape[1] // HD):
        columns = slice(group * HD, (group + 1) * HD)
        scores = lax.dot_general(
            keys, q_ref[:, columns], (((1,), (1,)), ((), ())), preferred_element_type=jnp.float32
        )
        scores = jnp.where(live, scores * factor, -1e30)
        expo = jnp.exp2(scores - jnp.max(scores, axis=0, keepdims=True))
        denom = jnp.sum(expo, axis=0, keepdims=True)
        weights = (expo * (gain / denom)).astype(jnp.bfloat16)
        out_ref[:, columns] = lax.dot_general(
            weights, vals, (((0,), (0,)), ((), ())), preferred_element_type=jnp.float32
        ).astype(out_ref.dtype)


def body(queries, image_kv, visible, gate):
    sections = lax.axis_size("section")
    dps = lax.axis_size("dp")
    count = sections * dps
    img_dev, width = image_kv.shape[2:]
    heads = width // HD
    per_token = 2 * heads
    tokens = count * img_dev
    rows, columns = queries.shape[1:]
    block = columns // heads
    vmem = pl.BlockSpec(memory_space=pltpu.VMEM)
    gathered = pl.pallas_call(
        functools.partial(gather_kernel, sections, dps),
        out_shape=jax.ShapeDtypeStruct((per_token, tokens, HD), image_kv.dtype),
        in_specs=[vmem],
        out_specs=vmem,
        scratch_shapes=[
            pltpu.VMEM((sections, img_dev * per_token, HD), jnp.float32),
            pltpu.VMEM((sections, img_dev * per_token, HD), image_kv.dtype),
            pltpu.VMEM((count, img_dev * per_token, HD), image_kv.dtype),
            pltpu.VMEM((tokens * per_token, HD), jnp.float32),
            pltpu.SemaphoreType.DMA,
            pltpu.SemaphoreType.DMA,
        ],
        compiler_params=pltpu.CompilerParams(
            collective_id=0, has_side_effects=True, vmem_limit_bytes=40 * 1024 * 1024
        ),
        name="gather_kv",
    )(jnp.transpose(image_kv, (0, 2, 1, 3)))
    out = pl.pallas_call(
        attend_kernel,
        out_shape=jax.ShapeDtypeStruct((rows, columns), queries.dtype),
        grid=(heads,),
        in_specs=[
            pl.BlockSpec((rows, block), lambda k: (0, k)),
            pl.BlockSpec((per_token, tokens, HD), lambda k: (0, 0, 0)),
            pl.BlockSpec((1, rows), lambda k: (0, 0)),
            pl.BlockSpec((1, 1), lambda k: (0, 0)),
        ],
        out_specs=pl.BlockSpec((rows, block), lambda k: (0, k)),
        compiler_params=pltpu.CompilerParams(vmem_limit_bytes=40 * 1024 * 1024),
        name="attend",
    )(queries[0], gathered, visible.reshape(1, rows), gate.reshape(1, 1))
    return out[None]


def solution(mesh):
    in_specs = (
        P("section", "dp", None),
        P(None, None, ("section", "dp"), None),
        P("dp"),
        P("section"),
    )
    out_specs = P("section", "dp", None)
    return jax.shard_map(body, mesh=mesh, in_specs=in_specs, out_specs=out_specs, check_vma=False)
```

time: 55.1 us -> 32.8 us (0.60)
  blocking collectives: 31.4 us -> 0 us
  Pallas kernels: 0 us -> 28.9 us
  other arithmetic: 5.7 us -> 0 us
  local copies, waits for them, and re-layouts: 8.36 us -> 2.95 us
  starting transfers between devices: 4.24 us -> 0 us
  matrix products: 4.23 us -> 0 us
    all_gather x1 -> x0, blocking collectives: 31.4 us -> none  [body(): whole = lax.all_gather(mine, 'dp', axis=2, tiled=True)]
    pallas_call x0 -> x2, Pallas kernels: none -> 28.9 us  [the longest x1 17.5 us: body(): pl.pallas_call(attend_kernel, out_shape=jax.ShapeDtypeStruct((rows, colum...]
    reshape x1 -> x0, local copies, waits for them, and re-layouts: 5.63 us -> none  [body(): result = jnp.transpose(result, (2, 0, 1, 3)).reshape(rows, H * HD)]
    all_to_all x1 -> x0, starting transfers between devices: 4.24 us -> none  [body(): lax.all_to_all(image_kv, 'section', split_axis=0, concat_axis=2, tiled=True)]
    dot_general x2 -> x0, matrix products: 4.23 us -> none  [the longest x1 2.73 us: attend(): jnp.einsum('kgtn,nkd->kgtd', expo.astype(jnp.bfloat16), vals, preferred_e...]
    convert_element_type x1 -> x0, other arithmetic: 3.99 us -> none  [body(): return result.astype(jnp.bfloat16)[None]]
    unnamed x3 -> x6, local copies, waits for them, and re-layouts: 2.2 us -> 2.95 us
    lt x1 -> x0, other arithmetic: 0.73 us -> none  [attend(): live = glob[None, :] < seen[:, None]]
  transfers between devices with their start and end apart: 1 -> 0, of which waited for: 0 -> 0; matrix products, arithmetic and copies ran while one was open for 7% -> 0% of each run, Pallas kernels for 0% -> 0%
where the time goes in v1:
time: 32.8 us; the launch traced here: 32.5 us
  Pallas kernels  28.9 us (88%)
  local copies, waits for them, and re-layouts  2.95 us (9%)
  between operations  0.68 us (2%)
    pallas_call x1, Pallas kernels, body(): pl.pallas_call(attend_kernel, out_shape=jax.ShapeDtypeStruct((rows, colum...  17.5 us
    pallas_call x1, Pallas kernels, body(): pl.pallas_call(functools.partial(gather_kernel, sections, dps), out_shape...  11.3 us
    unnamed x6, local copies, waits for them, and re-layouts  2.95 us

profile of v1, /device:TPU:0, one launch (start us, length us, event | category | flops | bytes accessed | tf_op | source)
XLA Modules:
  0.0 32.5 jit_solution(2359083258566737653)
XLA Ops:
  0.7 0.0 copy-start.1
  0.7 0.7 %copy-done.1 = bf16[4,2,1,1024]{3,1,2,0:T(2,128)(2,1)S(1)} copy-done((bf16[4,2,1,1024]{3,1,2,0:T(2,128)(2,1)S(1)}, bf16[4,2,1,1024]{3,1,2,0:T(2,128)(2,1)}, u32[]{:S(2)}) %copy-start.1) | copy-done | bytes 16408
  1.4 11.3 %gather_kv.1.kv_ref = bf16[16,32,128]{2,1,0:T(8,128)(2,1)S(1)} custom-call(bf16[4,1,2,1024]{3,2,1,0:T(2,128)(2,1)S(1)} %bitcast.7), custom_call_target="tpu_custom_call" | custom-call | tf_op jit(solution)/shard_map/gather_kv/pallas_call | solution.py:108
  12.7 0.0 copy-start
  12.7 1.6 %copy-done = bf16[1,128,8192]{2,1,0:T(8,128)(2,1)S(1)} copy-done((bf16[1,128,8192]{2,1,0:T(8,128)(2,1)S(1)}, bf16[1,128,8192]{2,1,0:T(8,128)(2,1)}, u32[]{:S(2)}) %copy-start) | copy-done | bytes 2097176
  14.3 0.0 copy-start.2
  14.3 0.7 %copy-done.2 = s32[128]{0:T(128)S(1)} copy-done((s32[128]{0:T(128)S(1)}, s32[128]{0:T(128)}, u32[]{:S(2)}) %copy-start.2) | copy-done | bytes 536
  15.0 17.5 %attend.1 = bf16[128,8192]{1,0:T(8,128)(2,1)} custom-call(bf16[128,8192]{1,0:T(8,128)(2,1)S(1)} %bitcast.6, bf16[16,32,128]{2,1,0:T(8,128)(2,1)S(1)} %gather_kv.1.kv_ref, s32[1,128]{1,0:T(1,128)S(1)} %bitcast.8, f32[1,1]{1,0:T(1,128)} %bitcast.5.gate_ref), custom_call_target="tpu_custom_call" | custom-call | tf_op jit(solution)/shard_map/attend/pallas_call | solution.py:126
Async XLA Ops:
  0.7 0.7 %copy-start.1 = (bf16[4,2,1,1024]{3,1,2,0:T(2,128)(2,1)S(1)}, bf16[4,2,1,1024]{3,1,2,0:T(2,128)(2,1)}, u32[]{:S(2)}) copy-start(bf16[4,2,1,1024]{3,1,2,0:T(2,128)(2,1)} %param.5) | copy-start | bytes 49156
  12.7 1.6 %copy-start = (bf16[1,128,8192]{2,1,0:T(8,128)(2,1)S(1)}, bf16[1,128,8192]{2,1,0:T(8,128)(2,1)}, u32[]{:S(2)}) copy-start(bf16[1,128,8192]{2,1,0:T(8,128)(2,1)} %param.4) | copy-start | bytes 6291460
  14.3 0.7 %copy-start.2 = (s32[128]{0:T(128)S(1)}, s32[128]{0:T(128)}, u32[]{:S(2)}) copy-start(s32[128]{0:T(128)} %param.6) | copy-start | bytes 1540

commit v2 on v1

--- a/solution.py
+++ b/solution.py
@@ -9,6 +9,7 @@
 from jax.sharding import PartitionSpec as P
 
 HD = 128
+LANES = 128
 LOG2E = math.log2(math.e)
 
 
@@ -69,29 +70,49 @@
     pltpu.make_async_copy(others, others, send_sem).wait()
 
 
+def spread(block, pack):
+    zeros = jnp.zeros_like(block)
+    return jnp.concatenate(
+        [
+            jnp.concatenate([block if row == column else zeros for column in range(pack)], axis=1)
+            for row in range(pack)
+        ],
+        axis=0,
+    )
+
+
 def attend_kernel(q_ref, kv_ref, seen_ref, gate_ref, out_ref):
     head = pl.program_id(0)
     heads = kv_ref.shape[0] // 2
     tokens = kv_ref.shape[1]
     rows = q_ref.shape[0]
-    keys = kv_ref[head]
-    vals = kv_ref[heads + head]
+    pack = math.gcd(q_ref.shape[1] // HD, max(1, LANES // tokens))
+    width = pack * HD
+    keys = spread(kv_ref[head], pack)
+    vals = spread(kv_ref[heads + head], pack)
     seen = seen_ref[...]
     live = lax.broadcasted_iota(jnp.int32, (tokens, rows), 0) < seen
     gain = jnp.where(seen > 0, jnp.tanh(gate_ref[...]), 0.0)
     factor = LOG2E / math.sqrt(HD)
-    for group in range(q_ref.shape[1] // HD):
-        columns = slice(group * HD, (group + 1) * HD)
-        scores = lax.dot_general(
-            keys, q_ref[:, columns], (((1,), (1,)), ((), ())), preferred_element_type=jnp.float32
+    spans = [slice(at, at + width) for at in range(0, q_ref.shape[1], width)]
+    raw = [
+        lax.dot_general(
+            q_ref[:, span], keys, (((1,), (1,)), ((), ())), preferred_element_type=jnp.float32
         )
-        scores = jnp.where(live, scores * factor, -1e30)
-        expo = jnp.exp2(scores - jnp.max(scores, axis=0, keepdims=True))
-        denom = jnp.sum(expo, axis=0, keepdims=True)
-        weights = (expo * (gain / denom)).astype(jnp.bfloat16)
-        out_ref[:, columns] = lax.dot_general(
-            weights, vals, (((0,), (0,)), ((), ())), preferred_element_type=jnp.float32
-        ).astype(out_ref.dtype)
+        for span in spans
+    ]
+    turned = [scores.T for scores in raw]
+    weights = []
+    for scores in turned:
+        parts = []
+        for at in range(0, pack * tokens, tokens):
+            part = jnp.where(live, scores[at : at + tokens] * factor, -1e30)
+            expo = jnp.exp2(part - jnp.max(part, axis=0, keepdims=True))
+            denom = jnp.sum(expo, axis=0, keepdims=True)
+            parts.append(expo * (gain / denom))
+        weights.append(jnp.concatenate(parts, axis=0).T.astype(jnp.bfloat16))
+    for span, part in zip(spans, weights):
+        out_ref[:, span] = jnp.dot(part, vals, preferred_element_type=jnp.float32).astype(out_ref.dtype)
 
 
 def body(queries, image_kv, visible, gate):
@@ -119,7 +140,7 @@
             pltpu.SemaphoreType.DMA,
         ],
         compiler_params=pltpu.CompilerParams(
-            collective_id=0, has_side_effects=True, vmem_limit_bytes=40 * 1024 * 1024
+            collective_id=0, has_side_effects=True, vmem_limit_bytes=32 * 1024 * 1024
         ),
         name="gather_kv",
     )(jnp.transpose(image_kv, (0, 2, 1, 3)))
@@ -134,7 +155,7 @@
             pl.BlockSpec((1, 1), lambda k: (0, 0)),
         ],
         out_specs=pl.BlockSpec((rows, block), lambda k: (0, k)),
-        compiler_params=pltpu.CompilerParams(vmem_limit_bytes=40 * 1024 * 1024),
+        compiler_params=pltpu.CompilerParams(vmem_limit_bytes=60 * 1024 * 1024),
         name="attend",
     )(queries[0], gathered, visible.reshape(1, rows), gate.reshape(1, 1))
     return out[None]

time: 32.8 us -> 21.5 us (0.66)
  Pallas kernels: 28.9 us -> 19.2 us
  local copies, waits for them, and re-layouts: 2.95 us -> 1.34 us
    pallas_call x1, Pallas kernels: 17.5 us -> 7.82 us  [body(): pl.pallas_call(attend_kernel, out_shape=jax.ShapeDtypeStruct((rows, colum...]
    unnamed x6 -> x4, local copies, waits for them, and re-layouts: 2.95 us -> 1.34 us
where the time goes in v2:
time: 21.5 us; the launch traced here: 21.2 us
  Pallas kernels  19.2 us (89%)
  local copies, waits for them, and re-layouts  1.34 us (6%)
  between operations  0.68 us (3%)
    pallas_call x1, Pallas kernels, body(): pl.pallas_call(functools.partial(gather_kernel, sections, dps), out_shape...  11.3 us
    pallas_call x1, Pallas kernels, body(): pl.pallas_call(attend_kernel, out_shape=jax.ShapeDtypeStruct((rows, colum...  7.82 us
    unnamed x4, local copies, waits for them, and re-layouts  1.34 us

profile of v2, /device:TPU:0, one launch (start us, length us, event | category | flops | bytes accessed | tf_op | source)
XLA Modules:
  0.0 21.2 jit_solution(14748591288338977451)
XLA Ops:
  0.7 0.0 copy-start.1
  0.7 0.7 %copy-done.1 = bf16[4,2,1,1024]{3,1,2,0:T(2,128)(2,1)S(1)} copy-done((bf16[4,2,1,1024]{3,1,2,0:T(2,128)(2,1)S(1)}, bf16[4,2,1,1024]{3,1,2,0:T(2,128)(2,1)}, u32[]{:S(2)}) %copy-start.1) | copy-done | bytes 16408
  1.4 11.3 %gather_kv.1.kv_ref = bf16[16,32,128]{2,1,0:T(8,128)(2,1)S(1)} custom-call(bf16[4,1,2,1024]{3,2,1,0:T(2,128)(2,1)S(1)} %bitcast.6), custom_call_target="tpu_custom_call" | custom-call | tf_op jit(solution)/shard_map/gather_kv/pallas_call | solution.py:129
  12.7 0.0 copy-start
  12.7 0.6 %copy-done = bf16[16,32,128]{2,1,0:T(8,128)(2,1)} copy-done((bf16[16,32,128]{2,1,0:T(8,128)(2,1)}, bf16[16,32,128]{2,1,0:T(8,128)(2,1)S(1)}, u32[]{:S(2)}) %copy-start) | copy-done | bytes 131096
  13.4 7.8 %attend.1 = bf16[128,8192]{1,0:T(8,128)(2,1)} custom-call(bf16[128,8192]{1,0:T(8,128)(2,1)} %bitcast.7, bf16[16,32,128]{2,1,0:T(8,128)(2,1)} %copy-done, s32[1,128]{1,0:T(1,128)} %bitcast.8, f32[1,1]{1,0:T(1,128)} %bitcast.5.gate_ref), custom_call_target="tpu_custom_call" | custom-call | tf_op jit(solution)/shard_map/attend/pallas_call | solution.py:147
Async XLA Ops:
  0.7 0.7 %copy-start.1 = (bf16[4,2,1,1024]{3,1,2,0:T(2,128)(2,1)S(1)}, bf16[4,2,1,1024]{3,1,2,0:T(2,128)(2,1)}, u32[]{:S(2)}) copy-start(bf16[4,2,1,1024]{3,1,2,0:T(2,128)(2,1)} %param.5) | copy-start | bytes 49156
  12.7 0.6 %copy-start = (bf16[16,32,128]{2,1,0:T(8,128)(2,1)}, bf16[16,32,128]{2,1,0:T(8,128)(2,1)S(1)}, u32[]{:S(2)}) copy-start(bf16[16,32,128]{2,1,0:T(8,128)(2,1)S(1)} %gather_kv.1.kv_ref) | copy-start | bytes 393220

commit v3 on v2

v3 whole, which is shorter than its diff:
```python
import functools
import math

import jax
import jax.numpy as jnp
from jax import lax
from jax.experimental import pallas as pl
from jax.experimental.pallas import tpu as pltpu
from jax.sharding import PartitionSpec as P

HD = 128
LANES = 128
LOG2E = math.log2(math.e)


def gather_kernel(
    sections, dps, kv_ref, out_ref, held, stage, send, layer_kv, slots, wide, load_sem, send_sems, recv_sems
):
    my_section = lax.axis_index("section")
    my_dp = lax.axis_index("dp")
    img_dev = held.shape[1]
    heads = held.shape[3] // HD
    per_token = 2 * heads
    tokens = sections * dps * img_dev
    other_sections = [lax.rem(my_section + step, sections) for step in range(1, sections)]
    other_dps = [lax.rem(my_dp + step, dps) for step in range(1, dps)]

    load = pltpu.make_async_copy(kv_ref, held, load_sem)
    load.start()
    barrier = pltpu.get_barrier_semaphore()
    for dp in other_dps:
        pl.semaphore_signal(barrier, inc=1, device_id={"section": my_section, "dp": dp})
    for section in other_sections:
        pl.semaphore_signal(barrier, inc=1, device_id={"section": section, "dp": my_dp})
    load.wait()

    for layer in range(sections):
        for token in range(img_dev):
            rows = held[layer, token].astype(jnp.float32)
            for part in range(2):
                for head in range(heads):
                    at = token * per_token + part * heads + head
                    stage[layer, at : at + 1, :] = rows[part : part + 1, head * HD : (head + 1) * HD]
        send[layer] = stage[layer].astype(send.dtype)

    pl.semaphore_wait(barrier, sections + dps - 2)

    for section in other_sections:
        pltpu.make_async_remote_copy(
            src_ref=send.at[section],
            dst_ref=layer_kv.at[my_section],
            send_sem=send_sems.at[0],
            recv_sem=recv_sems.at[0],
            device_id={"section": section, "dp": my_dp},
        ).start()
    pltpu.make_async_copy(send.at[my_section], layer_kv.at[my_section], recv_sems.at[0]).start()
    pltpu.make_async_copy(layer_kv, layer_kv, recv_sems.at[0]).wait()

    mine = slots.at[:, my_dp]
    for dp in other_dps:
        pltpu.make_async_remote_copy(
            src_ref=layer_kv,
            dst_ref=mine,
            send_sem=send_sems.at[1],
            recv_sem=recv_sems.at[1],
            device_id={"section": my_section, "dp": dp},
        ).start()
    pltpu.make_async_copy(layer_kv, mine, recv_sems.at[1]).start()
    pltpu.make_async_copy(slots, slots, recv_sems.at[1]).wait()

    wide[...] = slots[...].reshape(tokens * per_token, HD).astype(jnp.float32)
    for row in range(per_token):
        out_ref[row] = wide[pl.ds(row, tokens, stride=per_token), :].astype(out_ref.dtype)

    sent = send.at[pl.ds(0, sections - 1)]
    pltpu.make_async_copy(sent, sent, send_sems.at[0]).wait()
    sent = slots.at[:, pl.ds(0, dps - 1)]
    pltpu.make_async_copy(sent, sent, send_sems.at[1]).wait()


def spread(block, pack):
    zeros = jnp.zeros_like(block)
    return jnp.concatenate(
        [
            jnp.concatenate([block if row == column else zeros for column in range(pack)], axis=1)
            for row in range(pack)
        ],
        axis=0,
    )


def attend_kernel(step_heads, q_ref, kv_ref, seen_ref, gate_ref, out_ref):
    heads = kv_ref.shape[0] // 2
    tokens = kv_ref.shape[1]
    rows, columns = q_ref.shape
    first = pl.program_id(0) * step_heads
    block = columns // step_heads
    pack = math.gcd(block // HD, max(1, LANES // tokens))
    width = pack * HD
    seen = seen_ref[...]
    live = lax.broadcasted_iota(jnp.int32, (tokens, rows), 0) < seen
    gain = jnp.where(seen > 0, jnp.tanh(gate_ref[...]), 0.0)
    factor = LOG2E / math.sqrt(HD)
    spans = [slice(at, at + width) for at in range(0, columns, width)]
    turned = []
    for head in range(step_heads):
        keys = spread(kv_ref[first + head], pack)
        for span in spans[head * (block // width) : (head + 1) * (block // width)]:
            scores = lax.dot_general(
                q_ref[:, span], keys, (((1,), (1,)), ((), ())), preferred_element_type=jnp.float32
            )
            turned.append(scores.T)
    weights = []
    for scores in turned:
        parts = []
        for at in range(0, pack * tokens, tokens):
            part = jnp.where(live, scores[at : at + tokens] * factor, -1e30)
            expo = jnp.exp2(part - jnp.max(part, axis=0, keepdims=True))
            denom = jnp.sum(expo, axis=0, keepdims=True)
            parts.append(expo * (gain / denom))
        weights.append(jnp.concatenate(parts, axis=0).T.astype(jnp.bfloat16))
    for head in range(step_heads):
        vals = spread(kv_ref[heads + first + head], pack)
        for at in range(head * (block // width), (head + 1) * (block // width)):
            out_ref[:, spans[at]] = jnp.dot(
                weights[at], vals, preferred_element_type=jnp.float32
            ).astype(out_ref.dtype)


def body(queries, image_kv, visible, gate):
    sections = lax.axis_size("section")
    dps = lax.axis_size("dp")
    count = sections * dps
    img_dev, width = image_kv.shape[2:]
    heads = width // HD
    per_token = 2 * heads
    tokens = count * img_dev
    rows, columns = queries.shape[1:]
    step_heads = math.gcd(heads, max(1, LANES // tokens))
    block = columns // heads * step_heads
    vmem = pl.BlockSpec(memory_space=pltpu.VMEM)
    gathered = pl.pallas_call(
        functools.partial(gather_kernel, sections, dps),
        out_shape=jax.ShapeDtypeStruct((per_token, tokens, HD), image_kv.dtype),
        in_specs=[pl.BlockSpec(memory_space=pl.ANY)],
        out_specs=vmem,
        scratch_shapes=[
            pltpu.VMEM((sections, img_dev, 2, width), image_kv.dtype),
            pltpu.VMEM((sections, img_dev * per_token, HD), jnp.float32),
            pltpu.VMEM((sections, img_dev * per_token, HD), image_kv.dtype),
            pltpu.VMEM((sections, img_dev * per_token, HD), image_kv.dtype),
            pltpu.VMEM((sections, dps, img_dev * per_token, HD), image_kv.dtype),
            pltpu.VMEM((tokens * per_token, HD), jnp.float32),
            pltpu.SemaphoreType.DMA,
            pltpu.SemaphoreType.DMA((2,)),
            pltpu.SemaphoreType.DMA((2,)),
        ],
        compiler_params=pltpu.CompilerParams(
            collective_id=0, has_side_effects=True, vmem_limit_bytes=60 * 1024 * 1024
        ),
        name="gather_kv",
    )(jnp.transpose(image_kv, (0, 2, 1, 3)))
    out = pl.pallas_call(
        functools.partial(attend_kernel, step_heads),
        out_shape=jax.ShapeDtypeStruct((rows, columns), queries.dtype),
        grid=(heads // step_heads,),
        in_specs=[
            pl.BlockSpec((rows, block), lambda k: (0, k)),
            pl.BlockSpec((per_token, tokens, HD), lambda k: (0, 0, 0)),
            pl.BlockSpec((1, rows), lambda k: (0, 0)),
            pl.BlockSpec((1, 1), lambda k: (0, 0)),
        ],
        out_specs=pl.BlockSpec((rows, block), lambda k: (0, k)),
        compiler_params=pltpu.CompilerParams(vmem_limit_bytes=60 * 1024 * 1024),
        name="attend",
    )(queries[0], gathered, visible.reshape(1, rows), gate.reshape(1, 1))
    return out[None]


def solution(mesh):
    in_specs = (
        P("section", "dp", None),
        P(None, None, ("section", "dp"), None),
        P("dp"),
        P("section"),
    )
    out_specs = P("section", "dp", None)
    return jax.shard_map(body, mesh=mesh, in_specs=in_specs, out_specs=out_specs, check_vma=False)
```

time: 21.5 us -> 18.2 us (0.85)
  Pallas kernels: 19.2 us -> 17.3 us
  local copies, waits for them, and re-layouts: 1.34 us -> 0 us
    pallas_call x1, Pallas kernels: 7.82 us -> 3.83 us  [body(): pl.pallas_call(functools.partial(attend_kernel, step_heads), out_shape=ja...]
    pallas_call x1, Pallas kernels: 11.3 us -> 13.4 us  [body(): pl.pallas_call(functools.partial(gather_kernel, sections, dps), out_shape...]
    unnamed x4 -> x0, local copies, waits for them, and re-layouts: 1.34 us -> none
where the time goes in v3:
time: 18.2 us; the launch traced here: 17.9 us
  Pallas kernels  17.3 us (95%)
  between operations  0.66 us (4%)
    pallas_call x1, Pallas kernels, body(): pl.pallas_call(functools.partial(gather_kernel, sections, dps), out_shape...  13.4 us
    pallas_call x1, Pallas kernels, body(): pl.pallas_call(functools.partial(attend_kernel, step_heads), out_shape=ja...  3.83 us

profile of v3, /device:TPU:0, one launch (start us, length us, event | category | flops | bytes accessed | tf_op | source)
XLA Modules:
  0.0 17.9 jit_solution(3165279356977293293)
XLA Ops:
  0.7 13.4 %gather_kv.1.kv_ref = bf16[16,32,128]{2,1,0:T(8,128)(2,1)} custom-call(bf16[4,1,2,1024]{3,2,1,0:T(2,128)(2,1)} %bitcast.7), custom_call_target="tpu_custom_call" | custom-call | tf_op jit(solution)/shard_map/gather_kv/pallas_call | solution.py:142
  14.1 3.8 %attend.1 = bf16[128,8192]{1,0:T(8,128)(2,1)} custom-call(bf16[128,8192]{1,0:T(8,128)(2,1)} %bitcast.6, bf16[16,32,128]{2,1,0:T(8,128)(2,1)} %gather_kv.1.kv_ref, s32[1,128]{1,0:T(1,128)} %bitcast.8, f32[1,1]{1,0:T(1,128)} %bitcast.5.gate_ref), custom_call_target="tpu_custom_call" | custom-call | tf_op jit(solution)/shard_map/attend/pallas_call | solution.py:163

commit v4 on v3

--- a/solution.py
+++ b/solution.py
@@ -14,7 +14,7 @@
 
 
 def gather_kernel(
-    sections, dps, kv_ref, out_ref, held, stage, send, layer_kv, slots, wide, load_sem, send_sems, recv_sems
+    sections, dps, kv_ref, out_ref, held, stage, send, slots, wide, load_sem, send_sem, recv_sem
 ):
     my_section = lax.axis_index("section")
     my_dp = lax.axis_index("dp")
@@ -22,16 +22,27 @@
     heads = held.shape[3] // HD
     per_token = 2 * heads
     tokens = sections * dps * img_dev
-    other_sections = [lax.rem(my_section + step, sections) for step in range(1, sections)]
-    other_dps = [lax.rem(my_dp + step, dps) for step in range(1, dps)]
+    dp_ring = [lax.rem(my_dp + step, dps) for step in range(dps)]
+
+    def for_peers(act):
+        def one_section(step, unused):
+            section = lax.rem(my_section + step, sections)
+            for dp in dp_ring:
+                act(section, dp)
+            return unused
+
+        lax.fori_loop(1, sections, one_section, 0)
+        for dp in dp_ring[1:]:
+            act(my_section, dp)
 
     load = pltpu.make_async_copy(kv_ref, held, load_sem)
     load.start()
     barrier = pltpu.get_barrier_semaphore()
-    for dp in other_dps:
-        pl.semaphore_signal(barrier, inc=1, device_id={"section": my_section, "dp": dp})
-    for section in other_sections:
-        pl.semaphore_signal(barrier, inc=1, device_id={"section": section, "dp": my_dp})
+    for_peers(
+        lambda section, dp: pl.semaphore_signal(
+            barrier, inc=1, device_id={"section": section, "dp": dp}
+        )
+    )
     load.wait()
 
     for layer in range(sections):
@@ -43,39 +54,27 @@
                     stage[layer, at : at + 1, :] = rows[part : part + 1, head * HD : (head + 1) * HD]
         send[layer] = stage[layer].astype(send.dtype)
 
-    pl.semaphore_wait(barrier, sections + dps - 2)
+    pl.semaphore_wait(barrier, sections * dps - 1)
 
-    for section in other_sections:
-        pltpu.make_async_remote_copy(
+    mine = slots.at[my_section * dps + my_dp]
+    for_peers(
+        lambda section, dp: pltpu.make_async_remote_copy(
             src_ref=send.at[section],
-            dst_ref=layer_kv.at[my_section],
-            send_sem=send_sems.at[0],
-            recv_sem=recv_sems.at[0],
-            device_id={"section": section, "dp": my_dp},
+            dst_ref=mine,
+            send_sem=send_sem,
+            recv_sem=recv_sem,
+            device_id={"section": section, "dp": dp},
         ).start()
-    pltpu.make_async_copy(send.at[my_section], layer_kv.at[my_section], recv_sems.at[0]).start()
-    pltpu.make_async_copy(layer_kv, layer_kv, recv_sems.at[0]).wait()
-
-    mine = slots.at[:, my_dp]
-    for dp in other_dps:
-        pltpu.make_async_remote_copy(
-            src_ref=layer_kv,
-            dst_ref=mine,
-            send_sem=send_sems.at[1],
-            recv_sem=recv_sems.at[1],
-            device_id={"section": my_section, "dp": dp},
-        ).start()
-    pltpu.make_async_copy(layer_kv, mine, recv_sems.at[1]).start()
-    pltpu.make_async_copy(slots, slots, recv_sems.at[1]).wait()
+    )
+    pltpu.make_async_copy(send.at[my_section], mine, recv_sem).start()
+    pltpu.make_async_copy(slots, slots, recv_sem).wait()
 
     wide[...] = slots[...].reshape(tokens * per_token, HD).astype(jnp.float32)
     for row in range(per_token):
         out_ref[row] = wide[pl.ds(row, tokens, stride=per_token), :].astype(out_ref.dtype)
 
-    sent = send.at[pl.ds(0, sections - 1)]
-    pltpu.make_async_copy(sent, sent, send_sems.at[0]).wait()
-    sent = slots.at[:, pl.ds(0, dps - 1)]
-    pltpu.make_async_copy(sent, sent, send_sems.at[1]).wait()
+    sent = slots.at[pl.ds(0, sections * dps - 1)]
+    pltpu.make_async_copy(sent, sent, send_sem).wait()
 
 
 def spread(block, pack):
@@ -148,12 +147,11 @@
             pltpu.VMEM((sections, img_dev, 2, width), image_kv.dtype),
             pltpu.VMEM((sections, img_dev * per_token, HD), jnp.float32),
             pltpu.VMEM((sections, img_dev * per_token, HD), image_kv.dtype),
-            pltpu.VMEM((sections, img_dev * per_token, HD), image_kv.dtype),
-            pltpu.VMEM((sections, dps, img_dev * per_token, HD), image_kv.dtype),
+            pltpu.VMEM((count, img_dev * per_token, HD), image_kv.dtype),
             pltpu.VMEM((tokens * per_token, HD), jnp.float32),
             pltpu.SemaphoreType.DMA,
-            pltpu.SemaphoreType.DMA((2,)),
-            pltpu.SemaphoreType.DMA((2,)),
+            pltpu.SemaphoreType.DMA,
+            pltpu.SemaphoreType.DMA,
         ],
         compiler_params=pltpu.CompilerParams(
             collective_id=0, has_side_effects=True, vmem_limit_bytes=60 * 1024 * 1024

time: 18.2 us -> 16.8 us (0.923)
  Pallas kernels: 17.3 us -> 15.9 us
    pallas_call x1, Pallas kernels: 13.4 us -> 12.1 us  [body(): pl.pallas_call(functools.partial(gather_kernel, sections, dps), out_shape...]
where the time goes in v4:
time: 16.8 us; the launch traced here: 16.6 us
  Pallas kernels  15.9 us (95%)
  between operations  0.66 us (4%)
    pallas_call x1, Pallas kernels, body(): pl.pallas_call(functools.partial(gather_kernel, sections, dps), out_shape...  12.1 us
    pallas_call x1, Pallas kernels, body(): pl.pallas_call(functools.partial(attend_kernel, step_heads), out_shape=ja...  3.81 us

profile of v4, /device:TPU:0, one launch (start us, length us, event | category | flops | bytes accessed | tf_op | source)
XLA Modules:
  0.0 16.6 jit_solution(10006294541732600351)
XLA Ops:
  0.7 12.1 %gather_kv.1.kv_ref = bf16[16,32,128]{2,1,0:T(8,128)(2,1)} custom-call(bf16[4,1,2,1024]{3,2,1,0:T(2,128)(2,1)} %bitcast.7), custom_call_target="tpu_custom_call" | custom-call | tf_op jit(solution)/shard_map/gather_kv/pallas_call | solution.py:141
  12.8 3.8 %attend.1 = bf16[128,8192]{1,0:T(8,128)(2,1)} custom-call(bf16[128,8192]{1,0:T(8,128)(2,1)} %bitcast.6, bf16[16,32,128]{2,1,0:T(8,128)(2,1)} %gather_kv.1.kv_ref, s32[1,128]{1,0:T(1,128)} %bitcast.8, f32[1,1]{1,0:T(1,128)} %bitcast.5.gate_ref), custom_call_target="tpu_custom_call" | custom-call | tf_op jit(solution)/shard_map/attend/pallas_call | solution.py:161
